TPU v7x, 32 devices: a whole 2x2x4 slice. The times are simulated.
32 devices in a mesh: dp: 16 (over z, y, x), tensor: 2 (over core).
Axes of the slice: x: 2, y: 2, z: 4, core: 2. Of those that a mesh axis runs over, the one named last changes fastest.
Arguments:
- tokens: bfloat16 [32768, 768], P('dp'), may hold values from -6 to 6
- lengths: int32 [64], P('dp'), may hold values from 64 to 512, as said below
- projections: bfloat16 [3, 768, 768], P(None, None, 'tensor'), may hold values from -0.21875 to 0.21875
- attention_bias: float32 [2, 768], P(None, 'tensor'), may hold values from -3 to 3
- output_weight: bfloat16 [768, 768], P('tensor'), may hold values from -1.75 to 1.75
- output_bias: float32 [768], replicated, may hold values from -3 to 3
- first_gain: float32 [768], replicated, may hold values from 0.4 to 1.6
- first_shift: float32 [768], replicated, may hold values from -3 to 3
- inner_weight: bfloat16 [768, 3072], P(None, 'tensor'), may hold values from -0.21875 to 0.21875
- inner_bias: float32 [3072], P('tensor'), may hold values from -3 to 3
- outer_weight: bfloat16 [3072, 768], P('tensor'), may hold values from -0.21875 to 0.21875
- outer_bias: float32 [768], replicated, may hold values from -3 to 3
- second_gain: float32 [768], replicated, may hold values from 0.4 to 1.6
- second_shift: float32 [768], replicated, may hold values from -3 to 3
- cotangent: bfloat16 [32768, 768], P('dp'), may hold values from -6 to 6
Outputs:
- layer_output: bfloat16 [32768, 768], P('dp')
- input_gradient: bfloat16 [32768, 768], P('dp')
- projections_gradient: float32 [3, 768, 768], P(None, None, 'tensor')
- attention_bias_gradient: float32 [2, 768], P(None, 'tensor')
- output_weight_gradient: float32 [768, 768], P('tensor')
- output_bias_gradient: float32 [768], replicated
- first_gain_gradient: float32 [768], replicated
- first_shift_gradient: float32 [768], replicated
- inner_weight_gradient: float32 [768, 3072], P(None, 'tensor')
- inner_bias_gradient: float32 [3072], P('tensor')
- outer_weight_gradient: float32 [3072, 768], P('tensor')
- outer_bias_gradient: float32 [768], replicated
- second_gain_gradient: float32 [768], replicated
- second_shift_gradient: float32 [768], replicated
Inputs may be any that keep to these rules, and one draw needn't show every extreme that they name: `lengths`: each sequence has 64 to 512 live tokens; one sequence has exactly 512.
All inputs are finite; a program needn't handle non-finite values.
Results may differ from a plain program's by a relative error of at most 0.023.
Values may be sent and summed in bfloat16 or wider, within the bound.
A program may use at most 192 MiB of HBM per device.

v0:
```python
import jax
import jax.numpy as jnp
from jax import lax
from jax.sharding import PartitionSpec as P

HEAD = 64


def layer_norm(values, gain_vector, shift_vector):
    centered = values - jnp.mean(values, axis=-1, keepdims=True)
    variance = jnp.mean(centered * centered, axis=-1, keepdims=True)
    inverse = lax.rsqrt(variance + 1e-06)
    normed = centered * inverse
    return (normed * gain_vector + shift_vector, normed, inverse)


def norm_backward(upstream, normed, inverse, gain_vector):
    scaled = upstream * gain_vector
    return inverse * (
        scaled
        - jnp.mean(scaled, axis=-1, keepdims=True)
        - normed * jnp.mean(scaled * normed, axis=-1, keepdims=True)
    )


def exact_gelu(values):
    return jax.nn.gelu(values, approximate=False)


def masked_scores(queries, keys_block, length_value):
    scores = jnp.einsum(
        "qhd,khd->hqk", queries, keys_block, preferred_element_type=jnp.float32
    ) * HEAD ** (-0.5)
    visible = jnp.arange(keys_block.shape[0], dtype=jnp.int32) < length_value
    return jnp.where(visible[None, None, :], scores, -1e30)


def attend(entry):
    queries, keys_block, values_block, length_value = entry
    scores = masked_scores(queries, keys_block, length_value)
    maximum = jnp.max(scores, axis=-1, keepdims=True)
    exponent = jnp.exp(scores - maximum)
    totals = jnp.sum(exponent, axis=-1, keepdims=True)
    weights_low = (exponent / totals).astype(jnp.bfloat16)
    mixed = jnp.einsum(
        "hqk,khd->qhd", weights_low, values_block, preferred_element_type=jnp.float32
    )
    return (mixed.astype(jnp.bfloat16), maximum + jnp.log(totals))


def attend_backward(entry):
    queries, keys_block, values_block, upstream, log_total, length_value = entry
    scores = masked_scores(queries, keys_block, length_value)
    weights_soft = jnp.exp(scores - log_total)
    grad_weights = jnp.einsum(
        "qhd,khd->hqk", upstream, values_block, preferred_element_type=jnp.float32
    )
    centre = jnp.sum(weights_soft * grad_weights, axis=-1, keepdims=True)
    grad_scores = (weights_soft * (grad_weights - centre)).astype(jnp.bfloat16)
    factor = HEAD ** (-0.5)
    grad_queries = (
        jnp.einsum("hqk,khd->qhd", grad_scores, keys_block, preferred_element_type=jnp.float32)
        * factor
    )
    grad_keys = (
        jnp.einsum("hqk,qhd->khd", grad_scores, queries, preferred_element_type=jnp.float32)
        * factor
    )
    grad_values = jnp.einsum(
        "hqk,qhd->khd",
        weights_soft.astype(jnp.bfloat16),
        upstream,
        preferred_element_type=jnp.float32,
    )
    return (grad_queries, grad_keys, grad_values)


def per_device(
    tokens,
    lengths,
    projections,
    attention_bias,
    output_weight,
    output_bias,
    first_gain,
    first_shift,
    inner_weight,
    inner_bias,
    outer_weight,
    outer_bias,
    second_gain,
    second_shift,
    cotangent,
):
    slot_count = lengths.shape[0]
    row_count = tokens.shape[0]
    slot_length = row_count // slot_count
    local_width = projections.shape[2]
    head_count = local_width // HEAD
    shaped = (slot_count, slot_length, head_count, HEAD)
    inputs = tokens.astype(jnp.float32)
    bias_rows = jnp.stack([attention_bias[0], jnp.zeros_like(attention_bias[0]), attention_bias[1]])
    projected = jnp.einsum("td,cde->cte", tokens, projections, preferred_element_type=jnp.float32)
    projected_low = (projected + bias_rows[:, None, :]).astype(jnp.bfloat16)
    queries = projected_low[0].reshape(shaped)
    keys_all = projected_low[1].reshape(shaped)
    values_all = projected_low[2].reshape(shaped)
    mixed, log_total = lax.map(attend, (queries, keys_all, values_all, lengths))
    mixed_low = mixed.reshape(row_count, local_width)
    attention = lax.psum(
        jnp.dot(mixed_low, output_weight, preferred_element_type=jnp.float32).astype(jnp.bfloat16),
        "tensor",
    ).astype(jnp.float32)
    first_out, first_normed, first_inverse = layer_norm(
        inputs + attention + output_bias, first_gain, first_shift
    )
    first_low = first_out.astype(jnp.bfloat16)
    before = jnp.dot(first_low, inner_weight, preferred_element_type=jnp.float32) + inner_bias
    after, gelu_pull = jax.vjp(exact_gelu, before)
    after_low = after.astype(jnp.bfloat16)
    feedforward = lax.psum(
        jnp.dot(after_low, outer_weight, preferred_element_type=jnp.float32).astype(jnp.bfloat16),
        "tensor",
    ).astype(jnp.float32)
    layer_output, second_normed, second_inverse = layer_norm(
        first_out + feedforward + outer_bias, second_gain, second_shift
    )
    upstream = cotangent.astype(jnp.float32)
    second_gain_gradient = jnp.sum(upstream * second_normed, axis=0)
    second_shift_gradient = jnp.sum(upstream, axis=0)
    grad_second = norm_backward(upstream, second_normed, second_inverse, second_gain)
    outer_bias_gradient = jnp.sum(grad_second, axis=0)
    grad_second_low = grad_second.astype(jnp.bfloat16)
    outer_weight_gradient = jnp.einsum(
        "tf,td->fd", after_low, grad_second_low, preferred_element_type=jnp.float32
    )
    grad_after = jnp.einsum(
        "td,fd->tf", grad_second_low, outer_weight, preferred_element_type=jnp.float32
    )
    (grad_before,) = gelu_pull(grad_after)
    grad_before_low = grad_before.astype(jnp.bfloat16)
    inner_bias_gradient = jnp.sum(grad_before_low.astype(jnp.float32), axis=0)
    inner_weight_gradient = jnp.einsum(
        "td,tf->df", first_low, grad_before_low, preferred_element_type=jnp.float32
    )
    back_first = lax.psum(
        jnp.einsum(
            "tf,df->td", grad_before_low, inner_weight, preferred_element_type=jnp.float32
        ).astype(jnp.bfloat16),
        "tensor",
    ).astype(jnp.float32)
    grad_first_out = grad_second + back_first
    first_gain_gradient = jnp.sum(grad_first_out * first_normed, axis=0)
    first_shift_gradient = jnp.sum(grad_first_out, axis=0)
    grad_first = norm_backward(grad_first_out, first_normed, first_inverse, first_gain)
    output_bias_gradient = jnp.sum(grad_first, axis=0)
    grad_first_low = grad_first.astype(jnp.bfloat16)
    output_weight_gradient = jnp.einsum(
        "tl,td->ld", mixed_low, grad_first_low, preferred_element_type=jnp.float32
    )
    grad_mixed = jnp.einsum(
        "td,ld->tl", grad_first_low, output_weight, preferred_element_type=jnp.float32
    ).astype(jnp.bfloat16)
    grad_queries, grad_keys, grad_values = lax.map(
        attend_backward,
        (queries, keys_all, values_all, grad_mixed.reshape(shaped), log_total, lengths),
    )
    grad_projected = jnp.stack([grad_queries, grad_keys, grad_values]).reshape(
        3, row_count, local_width
    )
    grad_projected_low = grad_projected.astype(jnp.bfloat16)
    grad_summed = jnp.sum(grad_projected_low.astype(jnp.float32), axis=1)
    attention_bias_gradient = jnp.stack([grad_summed[0], grad_summed[2]])
    projections_gradient = jnp.einsum(
        "td,cte->cde", tokens, grad_projected_low, preferred_element_type=jnp.float32
    )
    back_input = lax.psum(
        jnp.einsum(
            "cte,cde->td", grad_projected_low, projections, preferred_element_type=jnp.float32
        ).astype(jnp.bfloat16),
        "tensor",
    ).astype(jnp.float32)
    input_gradient = (grad_first + back_input).astype(jnp.bfloat16)
    (
        projections_gradient,
        attention_bias_gradient,
        output_weight_gradient,
        output_bias_gradient,
        first_gain_gradient,
        first_shift_gradient,
        inner_weight_gradient,
        inner_bias_gradient,
        outer_weight_gradient,
        outer_bias_gradient,
        second_gain_gradient,
        second_shift_gradient,
    ) = lax.psum(
        (
            projections_gradient,
            attention_bias_gradient,
            output_weight_gradient,
            output_bias_gradient,
            first_gain_gradient,
            first_shift_gradient,
            inner_weight_gradient,
            inner_bias_gradient,
            outer_weight_gradient,
            outer_bias_gradient,
            second_gain_gradient,
            second_shift_gradient,
        ),
        "dp",
    )
    return (
        layer_output.astype(jnp.bfloat16),
        input_gradient,
        projections_gradient,
        attention_bias_gradient,
        output_weight_gradient,
        output_bias_gradient,
        first_gain_gradient,
        first_shift_gradient,
        inner_weight_gradient,
        inner_bias_gradient,
        outer_weight_gradient,
        outer_bias_gradient,
        second_gain_gradient,
        second_shift_gradient,
    )


def solution(mesh):
    in_specs = (
        P("dp", None),
        P("dp"),
        P(None, None, "tensor"),
        P(None, "tensor"),
        P("tensor", None),
        P(),
        P(),
        P(),
        P(None, "tensor"),
        P("tensor"),
        P("tensor", None),
        P(),
        P(),
        P(),
        P("dp", None),
    )
    out_specs = (
        P("dp", None),
        P("dp", None),
        P(None, None, "tensor"),
        P(None, "tensor"),
        P("tensor", None),
        P(),
        P(),
        P(),
        P(None, "tensor"),
        P("tensor"),
        P("tensor", None),
        P(),
        P(),
        P(),
    )
    return jax.shard_map(
        per_device, mesh=mesh, in_specs=in_specs, out_specs=out_specs, check_vma=False
    )
```

profile of v0, /device:TPU:0, one launch (start us, length us, event | category | flops | bytes accessed | tf_op | source)
XLA Modules:
  0.0 840.6 jit_solution(17614791287883799962)
XLA Ops:
  8.3 6.7 fusion.69
  17.3 4.1 reshape_squeeze.9
  24.4 3.9 reshape_squeeze.10
  31.1 3.8 reshape_squeeze.11
  37.9 37.4 %while.26 = (s32[]{:T(128)}, bf16[4,512,6,64]{1,3,2,0:T(8,128)(2,1)}, f32[4,6,512,1]{2,1,3,0:T(8,128)}, bf16[4,512,6,64]{1,3,2,0:T(8,128)(2,1)}, s32[4]{0:T(128)...) while((s32[]{:T(128)}, bf16[4,512,6,64]{1,3,2,0:T(8,128)(2,1)}, ...), condition=%wide.region_3.4_spmd, body=%wide.region_0.3_spmd.sunk | while | flops 421721600 | bytes 20554340 | solution.py:108
  83.2 26.0 %all-reduce.8.cloned.1.call-done = bf16[2048,768]{1,0:T(8,128)(2,1)} async-done(((bf16[2048,768]{1,0:T(8,128)(2,1)}), bf16[2048,768]{1,0:T(8,128)(2,1)}) %all-reduce.8.cloned.1.call-update) | async-done | bytes 3145744 | tf_op jit(solution)/shard_map/psum | solution.py:110
  109.2 4.1 fusion.68
  116.2 34.4 %multiply_convert_fusion.1 = (bf16[2048,1536]{1,0:T(8,128)(2,1)S(1)}, f32[2048,1536]{1,0:T(8,128)}, f32[2048,1536]{1,0:T(8,128)}) fusion(f32[1536]{0:T(1024)S(1)} %copy-done.33, bf16[768,1536]{1,0:T(8,128)(2,1)S(1)} %copy-done, f32[768]{0:T(1024)S(1)} %copy-done.31, f32[768]{0:T(1024)S(1)} %copy-done.24, f32[2048]{0:T(1024)S(1)} %add_rsqrt_fusion.1, ...), kind=kOutput, calls=%fused_computation.65 | convolution fusion | flops 5053612032 | bytes 40139776 | tf_op jit(solution)/shard_map/dot_general | solution.py:118
  153.3 6.3 convolution_convert_fusion.2
  159.7 24.5 %all-reduce.10.cloned.1.call-done = bf16[2048,768]{1,0:T(8,128)(2,1)} async-done(((bf16[2048,768]{1,0:T(8,128)(2,1)}), bf16[2048,768]{1,0:T(8,128)(2,1)}) %all-reduce.10.cloned.1.call-update) | async-done | bytes 3145744 | tf_op jit(solution)/shard_map/psum | solution.py:121
  184.2 5.5 fusion.88
  195.3 5.1 fusion.64
  200.3 20.5 %convert_reduce_fusion = (f32[1536]{0:T(1024)}, bf16[2048,1536]{1,0:T(8,128)(2,1)}) fusion(f32[2048,1536]{1,0:T(8,128)} %get-tuple-element.233, bf16[1536,768]{1,0:T(8,128)(2,1)} %param.29, f32[2048,768]{1,0:T(8,128)} %get-tuple-element.238, f32[2048,1536]{1,0:T(8,128)} %get-tuple-element.247, f32[1536]{0:T(1024)S(1)} %copy-done.33), kind=kOutput, calls=%fused_computation.63 | convolution fusion | flops 4886886912 | bytes 40120320 | tf_op jit(solution)/shard_map/td,fd->tf/dot_general | solution.py:137
  220.8 9.3 %convolution_convert_fusion.1 = bf16[2048,768]{1,0:T(8,128)(2,1)} fusion(bf16[2048,1536]{1,0:T(8,128)(2,1)} %get-tuple-element.249, bf16[768,1536]{1,0:T(8,128)(2,1)S(1)} %copy-done), kind=kOutput, calls=%fused_computation.111 | convolution fusion | flops 4833411072 | bytes 11796480 | tf_op jit(solution)/shard_map/tf,df->td/dot_general | solution.py:147
  230.2 24.5 %all-reduce.12.cloned.1.call-done = bf16[2048,768]{1,0:T(8,128)(2,1)} async-done(((bf16[2048,768]{1,0:T(8,128)(2,1)}), bf16[2048,768]{1,0:T(8,128)(2,1)}) %all-reduce.12.cloned.1.call-update) | async-done | bytes 3145744 | tf_op jit(solution)/shard_map/psum | solution.py:146
  254.6 9.9 %multiply_reduce_fusion.1 = (f32[768]{0:T(1024)S(1)}, f32[2048]{0:T(1024)S(1)}, f32[2048]{0:T(1024)S(1)}, f32[768]{0:T(1024)S(1)}, f32[768]{0:T(1024)S(1)}) fusion(f32[2048,768]{1,0:T(8,128)} %get-tuple-element.238, bf16[2048,768]{1,0:T(8,128)(2,1)} %all-reduce.12.cloned.1.call-done, f32[2048]{0:T(1024)S(1)} %add_rsqrt_fusion.1, ...), kind=kLoop, calls=%fused_computation.92 | loop fusion | flops 25159424 | bytes 15776768 | tf_op jit(solution)/shard_map/reduce_sum | solution.py:153
  264.6 5.5 fusion.87
  278.6 3.8 reshape.125
  285.3 64.3 %while.27 = (s32[]{:T(128)}, bf16[4,512,6,64]{1,3,2,0:T(8,128)(2,1)}, bf16[4,512,6,64]{1,3,2,0:T(8,128)(2,1)}, bf16[4,512,6,64]{1,3,2,0:T(8,128)(2,1)}, bf16[4,5...) while((s32[]{:T(128)}, ...), condition=%wide.region_17.18_spmd, body=%wide.region_15.17_spmd.sunk | while | flops 1030616576 | bytes 83856648 | solution.py:164
  356.4 3.8 copy.61
  360.2 3.8 stack.20
  370.4 3.8 stack.21
  376.9 8.4 %bitcast_convert_fusion = bf16[2048,768]{1,0:T(8,128)(2,1)} fusion(bf16[3,768,384]{2,1,0:T(8,128)(2,1)} %param.21, bf16[1,2048,384]{2,1,0:T(8,128)(2,1)} %copy.65, bf16[1,2048,384]{2,1,0:T(8,128)(2,1)} %copy.64, bf16[1,2048,384]{2,1,0:T(8,128)(2,1)S(1)} %copy.63), kind=kOutput, calls=%fused_computation.91 | convolution fusion | flops 3630170112 | bytes 9633792 | tf_op jit(solution)/shard_map/cte,cde->td/dot_general | solution.py:178
  385.5 12.5 %fusion.82 = f32[768,1536]{1,0:T(8,128)} fusion(bf16[2048,1536]{1,0:T(8,128)(2,1)} %get-tuple-element.249, f32[768]{0:T(1024)S(1)} %copy-done.31, f32[768]{0:T(1024)S(1)} %copy-done.24, bf16[2048,768]{1,0:T(8,128)(2,1)} %all-reduce.8.cloned.1.call-done, bf16[2048,768]{1,0:T(8,128)(2,1)} %param.19, f32[2048]{0:T(1024)S(1)} %add_rsqrt_fusion.1, ...), kind=kOutput, calls=%fused_computation.124 | convolution fusion | flops 4845993984 | bytes 17327104 | tf_op jit(solution)/shard_map/td,tf->df/dot_general | solution.py:143
  398.0 10.8 %fusion.79 = f32[1536,768]{1,0:T(8,128)} fusion(bf16[2048,1536]{1,0:T(8,128)(2,1)} %copy-done.36, f32[2048,768]{1,0:T(8,128)} %get-tuple-element.238), kind=kOutput, calls=%fused_computation.121 | convolution fusion | flops 4833411072 | bytes 17301504 | tf_op jit(solution)/shard_map/tf,td->fd/dot_general | solution.py:134
  408.8 5.3 fusion.76
  414.2 5.8 fusion.73
  422.2 81.5 %all-reduce = (f32[2,384]{1,0:T(2,128)}, f32[768]{0:T(1024)}, f32[768]{0:T(1024)}, f32[768]{0:T(1024)}, f32[1536]{0:T(1024)}, /*index=5*/f32[768]{0:T(1024)}, f32[768]{0:T(1024)}, f32[768]{0:T(1024)}) all-reduce(f32[2,384]{1,0:T(2,128)S(1)} %pad_maximum_fusion.2, ...), channel_id=1, replica_groups=mesh['dp'=16,'tensor'=2] {'dp'}, use_global_device_ids=true, to_apply=%region_21.22 | all-reduce | flops 6912 | bytes 55296 | tf_op jit(solution)/shard_map/psum | solution.py:197
  503.7 6.4 add_convert_fusion.2
  510.1 309.7 %all-reduce.16.cloned.1.call-done = (f32[3,768,384]{1,2,0:T(8,128)}, f32[384,768]{1,0:T(8,128)}, f32[768,1536]{1,0:T(8,128)}, f32[1536,768]{1,0:T(8,128)}) async-done(((f32[3,768,384]{1,2,0:T(8,128)}, f32[384,768]{1,0:T(8,128)}, f32[768,1536]{1,0:T(8,128)}, f32[1536,768]{1,0:T(8,128)}), (f32[3,768,384]{1,2,0:T(8,128)}, f32[384,768]{1,0:T(8,128)}, f32[768,1536]{1,0:T(8,128)}, ...) | async-done | bytes 14155792 | tf_op jit(solution)/shard_map/psum | solution.py:197
  819.9 5.2 copy.67
  826.1 5.5 copy.112
  (219 shorter events, 165.2 us)
Async XLA Ops:
  7.2 109.0 %copy-start = (bf16[768,1536]{1,0:T(8,128)(2,1)S(1)}, bf16[768,1536]{1,0:T(8,128)(2,1)}, u32[]{:S(2)}) copy-start(bf16[768,1536]{1,0:T(8,128)(2,1)} %param.27) | copy-start | bytes 7077892
  7.2 102.0 %all-reduce.8.cloned.1.call-start = ((), (), s32[]{:S(2)}) async-start(), calls=%async_computation | async-start | bytes 6291456 | tf_op jit(solution)/shard_map/psum | solution.py:110
  24.4 13.5 %copy-start.34 = (s32[4]{0:T(128)S(1)}, s32[4]{0:T(128)}, u32[]{:S(2)}) copy-start(s32[4]{0:T(128)} %param.20) | copy-start | bytes 52
  75.3 4.3 copy-start.21
  78.4 30.7 %copy-start.23 = (f32[768]{0:T(1024)S(1)}, f32[768]{0:T(1024)}, u32[]{:S(2)}) copy-start(f32[768]{0:T(1024)} %param.24) | copy-start | bytes 9220
  83.1 33.1 %copy-start.24 = (f32[768]{0:T(1024)S(1)}, f32[768]{0:T(1024)}, u32[]{:S(2)}) copy-start(f32[768]{0:T(1024)} %param.25) | copy-start | bytes 9220
  83.1 33.1 %copy-start.31 = (f32[768]{0:T(1024)S(1)}, f32[768]{0:T(1024)}, u32[]{:S(2)}) copy-start(f32[768]{0:T(1024)} %param.26) | copy-start | bytes 9220
  83.1 33.1 %copy-start.33 = (f32[1536]{0:T(1024)S(1)}, f32[1536]{0:T(1024)}, u32[]{:S(2)}) copy-start(f32[1536]{0:T(1024)} %param.28) | copy-start | bytes 18436
  83.1 101.1 %all-reduce.10.cloned.1.call-start = ((), (), s32[]{:S(2)}) async-start(), calls=%async_computation.1 | async-start | bytes 6291456 | tf_op jit(solution)/shard_map/psum | solution.py:121
  109.2 4.7 copy-start.6
  116.2 37.1 %copy-start.32 = (bf16[1536,768]{1,0:T(8,128)(2,1)S(1)}, bf16[1536,768]{1,0:T(8,128)(2,1)}, u32[]{:S(2)}) copy-start(bf16[1536,768]{1,0:T(8,128)(2,1)} %param.29) | copy-start | bytes 7077892
  153.3 30.9 %copy-start.29 = (f32[768]{0:T(1024)S(1)}, f32[768]{0:T(1024)}, u32[]{:S(2)}) copy-start(f32[768]{0:T(1024)} %param.30) | copy-start | bytes 9220
  159.7 95.0 %all-reduce.12.cloned.1.call-start = ((), (), s32[]{:S(2)}) async-start(), calls=%async_computation.2 | async-start | bytes 6291456 | tf_op jit(solution)/shard_map/psum | solution.py:146
  190.6 4.6 copy-start.30
  230.1 273.6 %all-reduce.14.cloned.1.call-start = ((), (), s32[]{:S(2)}) async-start(), calls=%async_computation.3 | async-start | bytes 6291456 | tf_op jit(solution)/shard_map/psum | solution.py:177
  254.6 9.9 %copy-start.4 = (bf16[2048,768]{1,0:T(8,128)(2,1)S(1)}, bf16[2048,768]{1,0:T(8,128)(2,1)}, u32[]{:S(2)}) copy-start(bf16[2048,768]{1,0:T(8,128)(2,1)} %param.19) | copy-start | bytes 9437188
  254.6 9.9 %copy-start.7 = (bf16[2048,768]{1,0:T(8,128)(2,1)S(1)}, bf16[2048,768]{1,0:T(8,128)(2,1)}, u32[]{:S(2)}) copy-start(bf16[2048,768]{1,0:T(8,128)(2,1)} %all-reduce.8.cloned.1.call-done) | copy-start | bytes 9437188
  254.6 10.0 %copy-start.10 = (bf16[2048,768]{1,0:T(8,128)(2,1)S(1)}, bf16[2048,768]{1,0:T(8,128)(2,1)}, u32[]{:S(2)}) copy-start(bf16[2048,768]{1,0:T(8,128)(2,1)} %all-reduce.12.cloned.1.call-done) | copy-start | bytes 9437188
  264.6 8.2 copy-start.22
  275.8 9.5 %copy-start.8 = (bf16[4,512,6,64]{1,3,2,0:T(8,128)(2,1)S(1)}, bf16[4,512,6,64]{1,3,2,0:T(8,128)(2,1)}, u32[]{:S(2)}) copy-start(bf16[4,512,6,64]{1,3,2,0:T(8,128)(2,1)} %get-tuple-element.448) | copy-start | bytes 4718596
  275.8 9.5 %copy-start.35 = (s32[4]{0:T(128)S(1)}, s32[4]{0:T(128)}, u32[]{:S(2)}) copy-start(s32[4]{0:T(128)} %param.20) | copy-start | bytes 52
  285.3 4.1 copy-start.11
  333.5 4.1 copy-start.11
  385.4 434.5 %all-reduce.16.cloned.1.call-start = ((), (), s32[]{:S(2)}) async-start(), calls=%async_computation.4 | async-start | bytes 28311552 | tf_op jit(solution)/shard_map/psum | solution.py:197
  398.0 10.8 %copy-start.15 = (bf16[48,8,4,512]{3,1,2,0:T(8,128)(2,1)S(1)}, bf16[48,8,4,512]{3,1,2,0:T(8,128)(2,1)}, u32[]{:S(2)}) copy-start(bf16[48,8,4,512]{3,1,2,0:T(8,128)(2,1)} %copy-done.14) | copy-start | bytes 4718596
  408.8 5.4 copy-start.5
  408.8 5.4 copy-start.12
  408.8 5.4 copy-start.13
  819.9 5.3 copy-start.20
  825.1 6.5 slice-start
  826.1 5.5 slice-start.1
  826.1 7.7 copy-start.1
  (27 other events, 68.6 us)
Sparse Core Ops, SparseCore 0:
  83.2 25.8 all-reduce.7
  159.8 24.3 all-reduce.9
  230.2 24.3 all-reduce.11
  385.5 24.3 all-reduce.13
  420.1 399.7 all-reduce.15
where the time goes:
time: 846 us; the launch traced here: 841 us
  waiting for transfers between devices  385 us (46%)
  matrix products  194 us (23%)
  local copies, waits for them, and re-layouts  98.2 us (12%)
  blocking collectives  81.5 us (10%)
  other arithmetic  67.5 us (8%)
  between operations  14.4 us (2%)
    psum x1, waiting for transfers between devices, per_device(): lax.psum((projections_gradient, attention_bias_gradient, output_weight_gr...  310 us
    psum x1, blocking collectives, per_device(): lax.psum((projections_gradient, attention_bias_gradient, output_weight_gr...  81.5 us
    dot_general x1, matrix products, per_device(): jnp.dot(first_low, inner_weight, preferred_element_type=jnp.float32)  34.4 us
    psum x1, waiting for transfers between devices, per_device(): lax.psum(jnp.dot(mixed_low, output_weight, preferred_element_type=jnp.flo...  26 us
    psum x1, waiting for transfers between devices, per_device(): lax.psum(jnp.dot(after_low, outer_weight, preferred_element_type=jnp.floa...  24.5 us
    psum x1, waiting for transfers between devices, per_device(): lax.psum(jnp.einsum('tf,df->td', grad_before_low, inner_weight, preferred...  24.5 us
    unnamed x73, local copies, waits for them, and re-layouts  22.6 us
    dot_general x1, matrix products, per_device(): jnp.einsum('td,fd->tf', grad_second_low, outer_weight, preferred_element_...  20.5 us
  transfers between devices with their start and end apart: 5, of which 4 were waited for; matrix products, arithmetic and copies ran while one was open for 5% of the time, Pallas kernels for 0%

commit v1 on v0

--- a/solution.py
+++ b/solution.py
@@ -118,9 +118,14 @@
     before = jnp.dot(first_low, inner_weight, preferred_element_type=jnp.float32) + inner_bias
     after, gelu_pull = jax.vjp(exact_gelu, before)
     after_low = after.astype(jnp.bfloat16)
-    feedforward = lax.psum(
-        jnp.dot(after_low, outer_weight, preferred_element_type=jnp.float32).astype(jnp.bfloat16),
-        "tensor",
+    feedforward = jnp.sum(
+        lax.all_gather(
+            jnp.dot(after_low, outer_weight, preferred_element_type=jnp.float32).astype(
+                jnp.bfloat16
+            ),
+            "tensor",
+        ),
+        axis=0,
     ).astype(jnp.float32)
     layer_output, second_normed, second_inverse = layer_norm(
         first_out + feedforward + outer_bias, second_gain, second_shift

time: 846 us -> 846 us (level)
    psum x1 -> x0, waiting for transfers between devices: 24.5 us -> none  [per_device(): lax.psum(jnp.dot(after_low, outer_weight, preferred_element_type=jnp.floa...]
    all_gather x0 -> x1, waiting for transfers between devices: none -> 18 us  [per_device(): lax.all_gather(jnp.dot(after_low, outer_weight, preferred_element_type=jn...]
where the time goes in v1:
time: 846 us; the launch traced here: 841 us
  waiting for transfers between devices  378 us (45%)
  matrix products  194 us (23%)
  local copies, waits for them, and re-layouts  98.2 us (12%)
  blocking collectives  81.6 us (10%)
  other arithmetic  73.9 us (9%)
  between operations  14.4 us (2%)
    psum x1, waiting for transfers between devices, per_device(): lax.psum((projections_gradient, attention_bias_gradient, output_weight_gr...  310 us
    psum x1, blocking collectives, per_device(): lax.psum((projections_gradient, attention_bias_gradient, output_weight_gr...  81.6 us
    dot_general x1, matrix products, per_device(): jnp.dot(first_low, inner_weight, preferred_element_type=jnp.float32)  34.4 us
    psum x1, waiting for transfers between devices, per_device(): lax.psum(jnp.dot(mixed_low, output_weight, preferred_element_type=jnp.flo...  26 us
    psum x1, waiting for transfers between devices, per_device(): lax.psum(jnp.einsum('tf,df->td', grad_before_low, inner_weight, preferred...  24.5 us
    unnamed x73, local copies, waits for them, and re-layouts  22.6 us
    dot_general x1, matrix products, per_device(): jnp.einsum('td,fd->tf', grad_second_low, outer_weight, preferred_element_...  20.5 us
    dot_general x8, matrix products, masked_scores(): jnp.einsum('qhd,khd->hqk', queries, keys_block, preferred_element_type=jn...  19 us
  transfers between devices with their start and end apart: 5, of which 4 were waited for; matrix products, arithmetic and copies ran while one was open for 5% of the time, Pallas kernels for 0%

profile of v1, /device:TPU:0, one launch (start us, length us, event | category | flops | bytes accessed | tf_op | source)
XLA Modules:
  0.0 840.5 jit_solution(1629226203529718726)
XLA Ops:
  8.3 6.7 fusion.69
  17.3 4.1 reshape_squeeze.9
  24.4 3.9 reshape_squeeze.10
  31.1 3.8 reshape_squeeze.11
  37.9 37.4 %while.26 = (s32[]{:T(128)}, bf16[4,512,6,64]{1,3,2,0:T(8,128)(2,1)}, f32[4,6,512,1]{2,1,3,0:T(8,128)}, bf16[4,512,6,64]{1,3,2,0:T(8,128)(2,1)}, s32[4]{0:T(128)...) while((s32[]{:T(128)}, bf16[4,512,6,64]{1,3,2,0:T(8,128)(2,1)}, ...), condition=%wide.region_3.4_spmd, body=%wide.region_0.3_spmd.sunk | while | flops 421721600 | bytes 20554340 | solution.py:108
  83.2 26.0 %all-reduce.7.cloned.1.call-done = bf16[2048,768]{1,0:T(8,128)(2,1)} async-done(((bf16[2048,768]{1,0:T(8,128)(2,1)}), bf16[2048,768]{1,0:T(8,128)(2,1)}) %all-reduce.7.cloned.1.call-update) | async-done | bytes 3145744 | tf_op jit(solution)/shard_map/psum | solution.py:110
  109.2 4.1 fusion.68
  116.2 34.4 %multiply_convert_fusion.1 = (bf16[2048,1536]{1,0:T(8,128)(2,1)S(1)}, f32[2048,1536]{1,0:T(8,128)}, f32[2048,1536]{1,0:T(8,128)}) fusion(f32[1536]{0:T(1024)S(1)} %copy-done.33, bf16[768,1536]{1,0:T(8,128)(2,1)S(1)} %copy-done, f32[768]{0:T(1024)S(1)} %copy-done.31, f32[768]{0:T(1024)S(1)} %copy-done.24, f32[2048]{0:T(1024)S(1)} %add_rsqrt_fusion.1, ...), kind=kOutput, calls=%fused_computation.65 | convolution fusion | flops 5053612032 | bytes 40139776 | tf_op jit(solution)/shard_map/dot_general | solution.py:118
  153.3 6.3 convolution_convert_fusion.2
  159.7 18.0 %all-gather.3.cloned.1.call-done = bf16[4096,768]{1,0:T(8,128)(2,1)} async-done(((bf16[2048,768]{1,0:T(8,128)(2,1)}), bf16[4096,768]{1,0:T(8,128)(2,1)}) %all-gather.3.cloned.1.call-update) | async-done | bytes 6291472 | tf_op jit(solution)/shard_map/all_gather | solution.py:122
  177.8 6.4 reduce_sum.176
  184.1 5.5 fusion.88
  195.2 5.1 fusion.64
  200.2 20.5 %convert_reduce_fusion = (f32[1536]{0:T(1024)}, bf16[2048,1536]{1,0:T(8,128)(2,1)}) fusion(f32[2048,1536]{1,0:T(8,128)} %get-tuple-element.233, bf16[1536,768]{1,0:T(8,128)(2,1)} %param.29, f32[2048,768]{1,0:T(8,128)} %get-tuple-element.238, f32[2048,1536]{1,0:T(8,128)} %get-tuple-element.247, f32[1536]{0:T(1024)S(1)} %copy-done.33), kind=kOutput, calls=%fused_computation.63 | convolution fusion | flops 4886886912 | bytes 40120320 | tf_op jit(solution)/shard_map/td,fd->tf/dot_general | solution.py:142
  220.7 9.3 %convolution_convert_fusion.1 = bf16[2048,768]{1,0:T(8,128)(2,1)} fusion(bf16[2048,1536]{1,0:T(8,128)(2,1)} %get-tuple-element.249, bf16[768,1536]{1,0:T(8,128)(2,1)S(1)} %copy-done), kind=kOutput, calls=%fused_computation.111 | convolution fusion | flops 4833411072 | bytes 11796480 | tf_op jit(solution)/shard_map/tf,df->td/dot_general | solution.py:152
  230.1 24.5 %all-reduce.9.cloned.1.call-done = bf16[2048,768]{1,0:T(8,128)(2,1)} async-done(((bf16[2048,768]{1,0:T(8,128)(2,1)}), bf16[2048,768]{1,0:T(8,128)(2,1)}) %all-reduce.9.cloned.1.call-update) | async-done | bytes 3145744 | tf_op jit(solution)/shard_map/psum | solution.py:151
  254.5 9.9 %multiply_reduce_fusion.1 = (f32[768]{0:T(1024)S(1)}, f32[2048]{0:T(1024)S(1)}, f32[2048]{0:T(1024)S(1)}, f32[768]{0:T(1024)S(1)}, f32[768]{0:T(1024)S(1)}) fusion(f32[2048,768]{1,0:T(8,128)} %get-tuple-element.238, bf16[2048,768]{1,0:T(8,128)(2,1)} %all-reduce.9.cloned.1.call-done, f32[2048]{0:T(1024)S(1)} %add_rsqrt_fusion.1, ...), kind=kLoop, calls=%fused_computation.92 | loop fusion | flops 25159424 | bytes 15776768 | tf_op jit(solution)/shard_map/reduce_sum | solution.py:158
  264.5 5.5 fusion.87
  278.5 3.8 reshape.125
  285.2 64.3 %while.27 = (s32[]{:T(128)}, bf16[4,512,6,64]{1,3,2,0:T(8,128)(2,1)}, bf16[4,512,6,64]{1,3,2,0:T(8,128)(2,1)}, bf16[4,512,6,64]{1,3,2,0:T(8,128)(2,1)}, bf16[4,5...) while((s32[]{:T(128)}, ...), condition=%wide.region_17.18_spmd, body=%wide.region_15.17_spmd.sunk | while | flops 1030616576 | bytes 83856648 | solution.py:169
  360.1 3.8 stack.20
  370.3 3.8 stack.21
  376.9 8.4 %bitcast_convert_fusion = bf16[2048,768]{1,0:T(8,128)(2,1)} fusion(bf16[3,768,384]{2,1,0:T(8,128)(2,1)} %param.21, bf16[1,2048,384]{2,1,0:T(8,128)(2,1)} %copy.65, bf16[1,2048,384]{2,1,0:T(8,128)(2,1)} %copy.64, bf16[1,2048,384]{2,1,0:T(8,128)(2,1)S(1)} %copy.63), kind=kOutput, calls=%fused_computation.91 | convolution fusion | flops 3630170112 | bytes 9633792 | tf_op jit(solution)/shard_map/cte,cde->td/dot_general | solution.py:183
  385.4 12.5 %fusion.82 = f32[768,1536]{1,0:T(8,128)} fusion(bf16[2048,1536]{1,0:T(8,128)(2,1)} %get-tuple-element.249, f32[768]{0:T(1024)S(1)} %copy-done.31, f32[768]{0:T(1024)S(1)} %copy-done.24, bf16[2048,768]{1,0:T(8,128)(2,1)} %all-reduce.7.cloned.1.call-done, bf16[2048,768]{1,0:T(8,128)(2,1)} %param.19, f32[2048]{0:T(1024)S(1)} %add_rsqrt_fusion.1, ...), kind=kOutput, calls=%fused_computation.124 | convolution fusion | flops 4845993984 | bytes 17327104 | tf_op jit(solution)/shard_map/td,tf->df/dot_general | solution.py:148
  397.9 10.8 %fusion.79 = f32[1536,768]{1,0:T(8,128)} fusion(bf16[2048,1536]{1,0:T(8,128)(2,1)} %copy-done.36, f32[2048,768]{1,0:T(8,128)} %get-tuple-element.238), kind=kOutput, calls=%fused_computation.121 | convolution fusion | flops 4833411072 | bytes 17301504 | tf_op jit(solution)/shard_map/tf,td->fd/dot_general | solution.py:139
  408.7 5.3 fusion.76
  414.1 5.8 fusion.73
  422.1 81.6 %all-reduce = (f32[2,384]{1,0:T(2,128)}, f32[768]{0:T(1024)}, f32[768]{0:T(1024)}, f32[768]{0:T(1024)}, f32[1536]{0:T(1024)}, /*index=5*/f32[768]{0:T(1024)}, f32[768]{0:T(1024)}, f32[768]{0:T(1024)}) all-reduce(f32[2,384]{1,0:T(2,128)S(1)} %pad_maximum_fusion.2, ...), channel_id=1, replica_groups=mesh['dp'=16,'tensor'=2] {'dp'}, use_global_device_ids=true, to_apply=%region_21.22 | all-reduce | flops 6912 | bytes 55296 | tf_op jit(solution)/shard_map/psum | solution.py:202
  503.7 6.4 add_convert_fusion.2
  510.1 309.7 %all-reduce.13.cloned.1.call-done = (f32[3,768,384]{1,2,0:T(8,128)}, f32[384,768]{1,0:T(8,128)}, f32[768,1536]{1,0:T(8,128)}, f32[1536,768]{1,0:T(8,128)}) async-done(((f32[3,768,384]{1,2,0:T(8,128)}, f32[384,768]{1,0:T(8,128)}, f32[768,1536]{1,0:T(8,128)}, f32[1536,768]{1,0:T(8,128)}), (f32[3,768,384]{1,2,0:T(8,128)}, f32[384,768]{1,0:T(8,128)}, f32[768,1536]{1,0:T(8,128)}, ...) | async-done | bytes 14155792 | tf_op jit(solution)/shard_map/psum | solution.py:202
  819.8 5.2 copy.67
  826.1 5.5 copy.111
  (220 shorter events, 169.0 us)
Async XLA Ops:
  7.2 109.0 %copy-start = (bf16[768,1536]{1,0:T(8,128)(2,1)S(1)}, bf16[768,1536]{1,0:T(8,128)(2,1)}, u32[]{:S(2)}) copy-start(bf16[768,1536]{1,0:T(8,128)(2,1)} %param.27) | copy-start | bytes 7077892
  7.2 102.0 %all-reduce.7.cloned.1.call-start = ((), (), s32[]{:S(2)}) async-start(), calls=%async_computation | async-start | bytes 6291456 | tf_op jit(solution)/shard_map/psum | solution.py:110
  24.4 13.5 %copy-start.34 = (s32[4]{0:T(128)S(1)}, s32[4]{0:T(128)}, u32[]{:S(2)}) copy-start(s32[4]{0:T(128)} %param.20) | copy-start | bytes 52
  75.3 4.3 copy-start.21
  78.4 30.7 %copy-start.23 = (f32[768]{0:T(1024)S(1)}, f32[768]{0:T(1024)}, u32[]{:S(2)}) copy-start(f32[768]{0:T(1024)} %param.24) | copy-start | bytes 9220
  83.1 33.1 %copy-start.24 = (f32[768]{0:T(1024)S(1)}, f32[768]{0:T(1024)}, u32[]{:S(2)}) copy-start(f32[768]{0:T(1024)} %param.25) | copy-start | bytes 9220
  83.1 33.1 %copy-start.31 = (f32[768]{0:T(1024)S(1)}, f32[768]{0:T(1024)}, u32[]{:S(2)}) copy-start(f32[768]{0:T(1024)} %param.26) | copy-start | bytes 9220
  83.1 33.1 %copy-start.33 = (f32[1536]{0:T(1024)S(1)}, f32[1536]{0:T(1024)}, u32[]{:S(2)}) copy-start(f32[1536]{0:T(1024)} %param.28) | copy-start | bytes 18436
  83.1 94.6 %all-gather.3.cloned.1.call-start = ((), (), s32[]{:S(2)}) async-start(), calls=%async_computation.3 | async-start | bytes 9437184 | tf_op jit(solution)/shard_map/all_gather | solution.py:122
  109.2 4.7 copy-start.6
  116.2 37.1 %copy-start.32 = (bf16[1536,768]{1,0:T(8,128)(2,1)S(1)}, bf16[1536,768]{1,0:T(8,128)(2,1)}, u32[]{:S(2)}) copy-start(bf16[1536,768]{1,0:T(8,128)(2,1)} %param.29) | copy-start | bytes 7077892
  159.6 24.5 %copy-start.29 = (f32[768]{0:T(1024)S(1)}, f32[768]{0:T(1024)}, u32[]{:S(2)}) copy-start(f32[768]{0:T(1024)} %param.30) | copy-start | bytes 9220
  159.7 94.9 %all-reduce.9.cloned.1.call-start = ((), (), s32[]{:S(2)}) async-start(), calls=%async_computation.1 | async-start | bytes 6291456 | tf_op jit(solution)/shard_map/psum | solution.py:151
  190.6 4.6 copy-start.30
  230.0 273.7 %all-reduce.11.cloned.1.call-start = ((), (), s32[]{:S(2)}) async-start(), calls=%async_computation.2 | async-start | bytes 6291456 | tf_op jit(solution)/shard_map/psum | solution.py:182
  254.5 9.9 %copy-start.4 = (bf16[2048,768]{1,0:T(8,128)(2,1)S(1)}, bf16[2048,768]{1,0:T(8,128)(2,1)}, u32[]{:S(2)}) copy-start(bf16[2048,768]{1,0:T(8,128)(2,1)} %param.19) | copy-start | bytes 9437188
  254.5 9.9 %copy-start.7 = (bf16[2048,768]{1,0:T(8,128)(2,1)S(1)}, bf16[2048,768]{1,0:T(8,128)(2,1)}, u32[]{:S(2)}) copy-start(bf16[2048,768]{1,0:T(8,128)(2,1)} %all-reduce.7.cloned.1.call-done) | copy-start | bytes 9437188
  254.5 10.0 %copy-start.10 = (bf16[2048,768]{1,0:T(8,128)(2,1)S(1)}, bf16[2048,768]{1,0:T(8,128)(2,1)}, u32[]{:S(2)}) copy-start(bf16[2048,768]{1,0:T(8,128)(2,1)} %all-reduce.9.cloned.1.call-done) | copy-start | bytes 9437188
  264.5 8.2 copy-start.22
  275.7 9.5 %copy-start.8 = (bf16[4,512,6,64]{1,3,2,0:T(8,128)(2,1)S(1)}, bf16[4,512,6,64]{1,3,2,0:T(8,128)(2,1)}, u32[]{:S(2)}) copy-start(bf16[4,512,6,64]{1,3,2,0:T(8,128)(2,1)} %get-tuple-element.448) | copy-start | bytes 4718596
  275.7 9.5 %copy-start.35 = (s32[4]{0:T(128)S(1)}, s32[4]{0:T(128)}, u32[]{:S(2)}) copy-start(s32[4]{0:T(128)} %param.20) | copy-start | bytes 52
  285.2 4.1 copy-start.11
  301.3 4.1 copy-start.11
  385.3 434.5 %all-reduce.13.cloned.1.call-start = ((), (), s32[]{:S(2)}) async-start(), calls=%async_computation.4 | async-start | bytes 28311552 | tf_op jit(solution)/shard_map/psum | solution.py:202
  397.9 10.8 %copy-start.15 = (bf16[48,8,4,512]{3,1,2,0:T(8,128)(2,1)S(1)}, bf16[48,8,4,512]{3,1,2,0:T(8,128)(2,1)}, u32[]{:S(2)}) copy-start(bf16[48,8,4,512]{3,1,2,0:T(8,128)(2,1)} %copy-done.14) | copy-start | bytes 4718596
  408.7 5.4 copy-start.5
  408.7 5.4 copy-start.12
  408.7 5.4 copy-start.13
  819.8 5.3 copy-start.20
  825.1 6.5 slice-start
  826.1 5.5 slice-start.1
  826.1 7.7 copy-start.1
  (27 other events, 68.6 us)
Sparse Core Ops, SparseCore 0:
  83.2 25.8 all-reduce.6
  159.8 17.9 all-gather.2
  230.1 24.3 all-reduce.8
  385.4 24.3 all-reduce.10
  420.0 399.7 all-reduce.12
